TPU v7x, 32 devices: a whole 2x2x4 slice. The times are simulated.
32 devices in a mesh: groups: 2 (over y), tok: 4 (over z), width: 2 (over x), sub: 2 (over core).
Axes of the slice: x: 2, y: 2, z: 4, core: 2. Of those that a mesh axis runs over, the one named last changes fastest.
Arguments:
- activation: float32 [3072, 8192], P(('groups', 'tok', 'sub'), 'width'), parts along dimension 0, may hold values from -6 to 6
- cotangent: float32 [3072, 8192], P(('groups', 'tok', 'sub'), 'width'), parts along dimension 0, may hold values from -6 to 6
- query_output_factor: bfloat16 [32, 32, 8192], P(('groups', 'tok'), 'sub', 'width'), parts along dimension 0, may hold values from -0.0625 to 0.0625
- query_input_factor: bfloat16 [32, 32, 8192], P(('groups', 'tok'), 'sub', 'width'), parts along dimension 0, may hold values from -0.01171875 to 0.01171875
- query_dest: int32 [32, 1], P(('groups', 'tok')), parts along dimension 0, may hold values from 0 to 3; in each aligned block of 4 rows (0 to 3, 4 to 7, ...) at most 2 rows name the same one
- query_cluster: int32 [32, 1], P(('groups', 'tok')), parts along dimension 0, may hold values from 0 to 1
- token_cluster: int32 [3072], P(('groups', 'tok')), parts along dimension 0, may hold values from 0 to 1
- token_count: int32 [16], P('groups'), parts along dimension 0, may hold values from 1 to 192, 1152 in all
Outputs:
- scores: float32 [3072, 16], P(('groups', 'tok', 'width', 'sub')), parts along dimension 0
There are 2 independent parts, one for each index of `groups`. A program takes and returns all parts, laid end to end along the dimension named above; each array names one. Nothing has to cross between parts.
Inputs may be any that keep to these rules, and one draw needn't show every extreme that they name: `query_dest`: each row names 1 tok index; among the 4 queries of one tok index no tok index is named more than 2 times, a bound that some block reaches. `token_count`: the live slots are the first ones of a device; some device has all 192 live.
All inputs are finite; a program needn't handle non-finite values.
Results may differ from a plain program's by a relative error of at most 0.0003.
Values may be sent and summed in bfloat16 or wider, within the bound.
A program may use at most 64 MiB of HBM per device.

v0:
```python
import jax
import jax.numpy as jnp
from jax import lax
from jax.sharding import PartitionSpec as P

CAP = 2
CL_DEV = 2


def from_partner(value, axis, bit):
    mask = 2**bit
    pairs = [(source, source ^ mask) for source in range(lax.axis_size(axis))]
    return lax.ppermute(value, axis, pairs)


def route_slots(dest, count):
    targets = jnp.arange(count, dtype=jnp.int32)
    onehot = (dest[:, :, None] == targets[None, None, :]).astype(jnp.int32)
    before = jnp.cumsum(onehot, axis=1) - onehot
    return jnp.sum(before * onehot, axis=2)


def on_device(
    activation,
    cotangent,
    query_output_factor,
    query_input_factor,
    query_dest,
    query_cluster,
    token_cluster,
    token_count,
):
    ntok = lax.axis_size("tok")
    nsub = lax.axis_size("sub")
    nwide = lax.axis_size("width")
    mine = lax.axis_index("tok")
    half = lax.axis_index("sub")
    column = lax.axis_index("width")
    local_q, topc = query_dest.shape
    rows_dev = activation.shape[0]
    block_rows = rows_dev * nsub
    share = block_rows // nwide
    slots = CAP * ntok
    targets = jnp.arange(ntok, dtype=jnp.int32)
    places = jnp.arange(CAP, dtype=jnp.int32)
    own_slot = route_slots(query_dest.reshape(1, local_q * topc), ntok).reshape(local_q, topc)
    picks = (query_dest[None, None, :, :] == targets[:, None, None, None]) & (
        own_slot[None, None, :, :] == places[None, :, None, None]
    )
    selection_mask = jnp.sum(picks.astype(jnp.int32), axis=3).astype(jnp.bfloat16)
    send_u = jnp.einsum(
        "nea,avq->nevq", selection_mask, query_output_factor, preferred_element_type=jnp.float32
    ).astype(jnp.bfloat16)
    send_v = jnp.einsum(
        "nea,avq->nevq", selection_mask, query_input_factor, preferred_element_type=jnp.float32
    ).astype(jnp.bfloat16)
    all_dest, all_clus = (
        lax.all_gather(query_dest, "tok", axis=0, tiled=True),
        lax.all_gather(query_cluster, "tok", axis=0, tiled=True),
    )
    src_slot = route_slots(all_dest.reshape(ntok, local_q * topc), ntok).reshape(
        ntok * local_q, topc
    )
    source = (jnp.arange(ntok * local_q, dtype=jnp.int32) // local_q)[:, None]
    position = src_slot * ntok + source
    arrived = all_dest == mine
    slot_ids = jnp.arange(slots, dtype=jnp.int32)
    cluster_agreement = (
        arrived[:, :, None] & (position[:, :, None] == slot_ids[None, None, :])
    ).astype(jnp.float32)
    slot_query = jnp.sum(cluster_agreement, axis=1).T
    cluster_ids = jnp.arange(CL_DEV, dtype=jnp.int32)
    cluster_indicator = (all_clus[:, :, None] == cluster_ids[None, None, :]).astype(jnp.float32)
    slot_cluster_label = jnp.einsum("ndy,ndu->yu", cluster_agreement, cluster_indicator)
    other_act, other_cot = from_partner((activation, cotangent), "sub", 0)
    first = half == 0
    acts_all = jnp.concatenate(
        [jnp.where(first, activation, other_act), jnp.where(first, other_act, activation)], axis=0
    )
    cots_all = jnp.concatenate(
        [jnp.where(first, cotangent, other_cot), jnp.where(first, other_cot, cotangent)], axis=0
    )
    got_u, got_v = (
        lax.all_to_all(send_u, "tok", split_axis=0, concat_axis=0, tiled=True),
        lax.all_to_all(send_v, "tok", split_axis=0, concat_axis=0, tiled=True),
    )
    gradient_portion = jnp.einsum(
        "tk,nmrk->tmnr",
        cots_all,
        got_u,
        precision=lax.Precision.HIGHEST,
        preferred_element_type=jnp.float32,
    )
    act_part = jnp.einsum(
        "tk,nmrk->tmnr",
        acts_all,
        got_v,
        precision=lax.Precision.HIGHEST,
        preferred_element_type=jnp.float32,
    )
    width_rows = gradient_portion.shape[0]
    items = gradient_portion.shape[1]
    grad_proj = gradient_portion.reshape(width_rows, items, -1)
    act_proj = act_part.reshape(width_rows, items, -1)
    grad_proj = grad_proj.reshape(block_rows, -1)
    act_proj = act_proj.reshape(block_rows, -1)
    grad_mine, act_mine = (
        lax.psum_scatter(grad_proj, "width", scatter_dimension=0, tiled=True),
        lax.psum_scatter(act_proj, "width", scatter_dimension=0, tiled=True),
    )
    product = jnp.sum((grad_mine * act_mine).reshape(share, CAP, ntok, -1), axis=3).reshape(
        share, slots
    )
    local_rows = column * share + jnp.arange(share, dtype=jnp.int32)
    row_device = mine * nsub + local_rows // rows_dev
    device_ids = jnp.arange(token_count.shape[0], dtype=jnp.int32)
    limits = jnp.sum(
        jnp.where(device_ids[None, :] == row_device[:, None], token_count[None, :], 0), axis=1
    )
    valid = (local_rows % rows_dev < limits).astype(jnp.float32)
    row_clusters = lax.dynamic_slice_in_dim(token_cluster, column * share, share, 0)
    row_onehot = (row_clusters[:, None] == cluster_ids[None, :]).astype(jnp.float32)
    agree = (
        jnp.dot(row_onehot, slot_cluster_label.T, preferred_element_type=jnp.float32)
        * valid[:, None]
    )
    portion_value = jnp.dot(
        product * agree,
        slot_query,
        precision=lax.Precision.HIGHEST,
        preferred_element_type=jnp.float32,
    )
    return lax.psum_scatter(portion_value, "sub", scatter_dimension=0, tiled=True)


def solution(mesh):
    placed = (
        P(("groups", "tok", "sub"), "width"),
        P(("groups", "tok", "sub"), "width"),
        P(("groups", "tok"), "sub", "width"),
        P(("groups", "tok"), "sub", "width"),
        P(("groups", "tok"), None),
        P(("groups", "tok"), None),
        P(("groups", "tok")),
        P("groups"),
    )
    return jax.shard_map(
        on_device,
        mesh=mesh,
        in_specs=placed,
        out_specs=P(("groups", "tok", "width", "sub"), None),
        check_vma=False,
    )
```

profile of v0, /device:TPU:0, one launch (start us, length us, event | category | flops | bytes accessed | tf_op | source)
XLA Modules:
  0.0 112.3 jit_solution(14422240424537967714)
XLA Ops:
  6.6 0.5 collective-permute-start
  7.1 0.7 fusion.32
  7.8 0.8 select_reduce_fusion.2
  8.7 0.7 iota_compare_fusion.7
  9.3 3.1 %convolution_convert_fusion.1 = bf16[4,2,16,4096]{3,1,2,0:T(2,128)(2,1)} fusion(bf16[4,16,4096]{2,1,0:T(8,128)(2,1)} %param.10, pred[2,4]{1,0:T(4,128)(4,1)S(1)} %iota_compare_fusion.8, pred[4,4]{1,0:T(4,128)(4,1)S(1)} %iota_compare_fusion.7), kind=kOutput, calls=%fused_computation.9 | convolution fusion | flops 4718688 | bytes 1572888 | tf_op jit(solution)/shard_map/nea,avq->nevq/dot_general | solution.py:51
  12.4 6.0 %all-to-all-start = ((bf16[4,2,16,4096]{3,1,2,0:T(2,128)(2,1)}), bf16[4,2,16,4096]{3,1,2,0:T(2,128)(2,1)S(1)}, u32[]{:S(2)}, u32[]{:S(2)}) async-start(bf16[4,2,16,4096]{3,1,2,0:T(2,128)(2,1)} %convolution_convert_fusion.1), calls=%async_computation | async-start | bytes 2097152 | tf_op jit(solution)/shard_map/all_to_all | solution.py:84
  18.5 0.6 dynamic-slice
  20.0 24.9 %all-reduce.2 = (s32[16]{0:T(128)S(1)}, s32[16]{0:T(128)S(1)}) all-reduce(s32[16]{0:T(128)S(1)} %bitcast_dynamic-update-slice_fusion.1, s32[16]{0:T(128)S(1)} %bitcast_dynamic-update-slice_fusion), channel_id=1, replica_groups=mesh['groups'=2,'tok'=4,'width'=2,'sub'=2] {'tok'}, use_global_device_ids=true, to_apply=%add | all-reduce | flops 32 | bytes 256
  45.6 2.1 %convolution_convert_fusion = bf16[4,2,16,4096]{3,1,2,0:T(2,128)(2,1)} fusion(bf16[4,16,4096]{2,1,0:T(8,128)(2,1)S(1)} %copy-done.3, pred[2,4]{1,0:T(4,128)(4,1)S(1)} %iota_compare_fusion.8, pred[4,4]{1,0:T(4,128)(4,1)S(1)} %iota_compare_fusion.7), kind=kOutput, calls=%fused_computation.8 | convolution fusion | flops 4718688 | bytes 1572888 | tf_op jit(solution)/shard_map/nea,avq->nevq/dot_general | solution.py:54
  47.7 4.2 %all-to-all-start.1 = ((bf16[4,2,16,4096]{3,1,2,0:T(2,128)(2,1)}), bf16[4,2,16,4096]{3,1,2,0:T(2,128)(2,1)}, u32[]{:S(2)}, u32[]{:S(2)}) async-start(bf16[4,2,16,4096]{3,1,2,0:T(2,128)(2,1)} %convolution_convert_fusion), calls=%async_computation.1 | async-start | bytes 2097152 | tf_op jit(solution)/shard_map/all_to_all | solution.py:85
  52.0 3.3 %broadcast_select_fusion.3 = (f32[192,4096]{1,0:T(8,128)S(1)}, f32[192,4096]{1,0:T(8,128)S(1)}) fusion(f32[192,4096]{1,0:T(8,128)} %param.9, f32[192,4096]{1,0:T(8,128)} %collective-permute-done, pred[]{:T(512)S(6)} %eq.194), kind=kLoop, calls=%fused_computation.13 | loop fusion | flops 1572864 | bytes 12582913 | tf_op jit(solution)/shard_map/jit(_where)/select_n | solution.py:81
  55.3 3.8 %fusion.7 = f32[384,2,4,16]{0,3,1,2:T(8,128)S(1)} fusion(f32[192,4096]{1,0:T(8,128)S(1)} %get-tuple-element.10, f32[192,4096]{1,0:T(8,128)S(1)} %get-tuple-element.9, bf16[4,2,16,4096]{3,1,2,0:T(2,128)(2,1)S(1)} %all-to-all-done), kind=kOutput, calls=%fused_computation.15 | convolution fusion | flops 2417491968 | bytes 7536640 | tf_op jit(solution)/shard_map/tk,nmrk->tmnr/dot_general | solution.py:87
  59.2 0.8 copy.26
  60.3 5.1 %broadcast_select_fusion.1 = (f32[192,4096]{1,0:T(8,128)S(1)}, f32[192,4096]{1,0:T(8,128)}) fusion(f32[192,4096]{1,0:T(8,128)} %param.8, f32[192,4096]{1,0:T(8,128)} %collective-permute-done.1, pred[]{:T(512)S(6)} %eq.194), kind=kLoop, calls=%fused_computation.11 | loop fusion | flops 1572864 | bytes 12582913 | tf_op jit(solution)/shard_map/jit(_where)/select_n | solution.py:78
  65.4 12.0 %all-to-all-done.1 = bf16[4,2,16,4096]{3,1,2,0:T(2,128)(2,1)} async-done(((bf16[4,2,16,4096]{3,1,2,0:T(2,128)(2,1)}), bf16[4,2,16,4096]{3,1,2,0:T(2,128)(2,1)}, u32[]{:S(2)}, u32[]{:S(2)}) %all-to-all-start.1) | async-done | bytes 1048608 | tf_op jit(solution)/shard_map/all_to_all | solution.py:85
  77.4 5.9 %fusion.6 = f32[384,2,4,16]{0,3,1,2:T(8,128)S(1)} fusion(f32[192,4096]{1,0:T(8,128)} %get-tuple-element.8, f32[192,4096]{1,0:T(8,128)S(1)} %get-tuple-element.7, bf16[4,2,16,4096]{3,1,2,0:T(2,128)(2,1)} %all-to-all-done.1), kind=kOutput, calls=%fused_computation.14 | convolution fusion | flops 2417491968 | bytes 7536640 | tf_op jit(solution)/shard_map/tk,nmrk->tmnr/dot_general | solution.py:94
  83.3 0.8 copy.28
  84.3 1.0 copy.27
  85.3 9.1 %reduce-scatter.12.cloned.1.call-done = f32[192,128]{1,0:T(8,128)} async-done(((f32[384,128]{1,0:T(8,128)}), f32[192,128]{1,0:T(8,128)}) %reduce-scatter.12.cloned.1.call-update) | async-done | bytes 98320
  94.4 1.0 copy.29
  95.4 0.3 fusion.8
  95.7 0.9 fusion.20
  96.7 7.6 %reduce-scatter.14.cloned.1.call-done = f32[96,16]{1,0:T(8,128)} async-done(((f32[192,16]{1,0:T(8,128)}), f32[96,16]{1,0:T(8,128)}) %reduce-scatter.14.cloned.1.call-update) | async-done | bytes 6160
  104.3 1.5 %copy.31 = f32[96,16]{0,1:T(8,128)} copy(f32[96,16]{1,0:T(8,128)} %reduce-scatter.14.cloned.1.call-done) | data formatting | bytes 12288
  (45 shorter events, 1.5 us)
Async XLA Ops:
  6.5 12.0 %copy-start.5 = (u32[32]{0:T(128)S(1)}, u32[32]{0:T(128)}, u32[]{:S(2)}) copy-start(u32[32]{0:T(128)} %constant.68) | copy-start | bytes 388
  6.5 13.3 %copy-start = (s32[4,1]{0,1:T(1,128)S(1)}, s32[4,1]{0,1:T(1,128)}, u32[]{:S(2)}) copy-start(s32[4,1]{0,1:T(1,128)} %param.12) | copy-start | bytes 52
  6.5 13.4 %copy-start.4 = (s32[4,1]{0,1:T(1,128)S(1)}, s32[4,1]{0,1:T(1,128)}, u32[]{:S(2)}) copy-start(s32[4,1]{0,1:T(1,128)} %param.13) | copy-start | bytes 52
  6.5 38.9 %copy-start.2 = (s32[384]{0:T(512)S(1)}, s32[384]{0:T(512)}, u32[]{:S(2)}) copy-start(s32[384]{0:T(512)} %param.14) | copy-start | bytes 4612
  6.5 39.0 %copy-start.1 = (s32[8]{0:T(128)S(1)}, s32[8]{0:T(128)}, u32[]{:S(2)}) copy-start(s32[8]{0:T(128)} %param.15) | copy-start | bytes 100
  6.5 39.1 %copy-start.3 = (bf16[4,16,4096]{2,1,0:T(8,128)(2,1)S(1)}, bf16[4,16,4096]{2,1,0:T(8,128)(2,1)}, u32[]{:S(2)}) copy-start(bf16[4,16,4096]{2,1,0:T(8,128)(2,1)} %param.11) | copy-start | bytes 1572868
  6.6 45.5 %collective-permute-start = (f32[192,4096]{1,0:T(8,128)}, f32[192,4096]{1,0:T(8,128)}, u32[]{:S(2)}, u32[]{:S(2)}) collective-permute-start(f32[192,4096]{1,0:T(8,128)} %param.9), channel_id=1, source_target_pairs={{0,1},{1,0},{2,3},{3,2},{4,5},{5,4},{6,7},{7,6},{8,9},{9,8},{10,11... | collective-permute-start | bytes 9437192 | tf_op jit(solution)/shard_map/ppermute | solution.py:13
  12.4 35.3 %all-to-all-start = ((bf16[4,2,16,4096]{3,1,2,0:T(2,128)(2,1)}), bf16[4,2,16,4096]{3,1,2,0:T(2,128)(2,1)S(1)}, u32[]{:S(2)}, u32[]{:S(2)}) async-start(bf16[4,2,16,4096]{3,1,2,0:T(2,128)(2,1)} %convolution_convert_fusion.1), calls=%async_computation | async-start | bytes 2097152 | tf_op jit(solution)/shard_map/all_to_all | solution.py:84
  18.5 41.8 %collective-permute-start.1 = (f32[192,4096]{1,0:T(8,128)}, f32[192,4096]{1,0:T(8,128)}, u32[]{:S(2)}, u32[]{:S(2)}) collective-permute-start(f32[192,4096]{1,0:T(8,128)} %param.8), channel_id=1, source_target_pairs={{0,1},{1,0},{2,3},{3,2},{4,5},{5,4},{6,7},{7,6},{8,9},{9,8},{10,11... | collective-permute-start | bytes 9437192 | tf_op jit(solution)/shard_map/ppermute | solution.py:13
  47.7 29.7 %all-to-all-start.1 = ((bf16[4,2,16,4096]{3,1,2,0:T(2,128)(2,1)}), bf16[4,2,16,4096]{3,1,2,0:T(2,128)(2,1)}, u32[]{:S(2)}, u32[]{:S(2)}) async-start(bf16[4,2,16,4096]{3,1,2,0:T(2,128)(2,1)} %convolution_convert_fusion), calls=%async_computation.1 | async-start | bytes 2097152 | tf_op jit(solution)/shard_map/all_to_all | solution.py:85
  52.0 32.3 %reduce-scatter.10.cloned.1.call-start = ((), (), s32[]{:S(2)}) async-start(), calls=%async_computation.5 | async-start | bytes 294912
  60.0 34.4 %reduce-scatter.12.cloned.1.call-start = ((), (), s32[]{:S(2)}) async-start(), calls=%async_computation.6 | async-start | bytes 294912
  84.2 20.2 %reduce-scatter.14.cloned.1.call-start = ((), (), s32[]{:S(2)}) async-start(), calls=%async_computation.7 | async-start | bytes 147456
Sparse Core Ops, SparseCore 0:
  60.1 12.2 reduce-scatter.9
  84.3 10.0 reduce-scatter.11
  96.8 7.4 reduce-scatter.13
where the time goes:
time: 113 us; the launch traced here: 112 us
  waiting for transfers between devices  28.9 us (26%)
  blocking collectives  24.9 us (22%)
  matrix products  16.1 us (14%)
  between operations  13.9 us (12%)
  starting transfers between devices  11.2 us (10%)
  other arithmetic  11.2 us (10%)
  local copies, waits for them, and re-layouts  6.15 us (5%)
    unnamed x1, blocking collectives  24.9 us
    unnamed x6, waiting for transfers between devices  16.8 us
    all_to_all x1, waiting for transfers between devices, on_device(): lax.all_to_all(send_v, 'tok', split_axis=0, concat_axis=0, tiled=True)  12 us
    all_to_all x1, starting transfers between devices, on_device(): lax.all_to_all(send_u, 'tok', split_axis=0, concat_axis=0, tiled=True)  6.02 us
    dot_general x1, matrix products, on_device(): jnp.einsum('tk,nmrk->tmnr', acts_all, got_v, precision=lax.Precision.HIGH...  5.87 us
    unnamed x22, local copies, waits for them, and re-layouts  5.86 us
    select_n x1, other arithmetic, on_device(): jnp.where(first, activation, other_act)  5.15 us
    all_to_all x1, starting transfers between devices, on_device(): lax.all_to_all(send_v, 'tok', split_axis=0, concat_axis=0, tiled=True)  4.25 us
  transfers between devices with their start and end apart: 7, of which 3 were waited for; matrix products, arithmetic and copies ran while one was open for 26% of the time, Pallas kernels for 0%

commit v1 on v0

v1 whole, which is shorter than its diff:
```python
import functools

import jax
import jax.numpy as jnp
from jax import lax
from jax.experimental import pallas as pl
from jax.experimental.pallas import tpu as pltpu
from jax.sharding import PartitionSpec as P

CAP = 2
MESH = pl.DeviceIdType.MESH


def kernel(
    ntok,
    nwide,
    nsub,
    chunks,
    act_hbm,
    cot_hbm,
    u_ref,
    v_ref,
    dest_ref,
    clus_ref,
    tc_ref,
    cnt_ref,
    out_ref,
    tokens,
    high,
    low,
    outbox,
    inbox,
    acc,
    parts,
    meta_out,
    meta_in,
    load_sem,
    tok_send,
    tok_recv,
    meta_send,
    meta_recv,
    fac_send,
    fac_recv,
    part_send,
    part_recv,
):
    mine = lax.axis_index("tok")
    column = lax.axis_index("width")
    half = lax.axis_index("sub")
    local_q, topc = dest_ref.shape
    rows_dev, depth = act_hbm.shape
    block_rows = rows_dev * nsub
    rank = u_ref.shape[1]
    lanes = meta_out.shape[1]
    piece = depth // chunks
    nquad = nwide * nsub
    quad = column * nsub + half
    share = block_rows // nquad
    sources = (cot_hbm, act_hbm)
    factors = (u_ref, v_ref)
    half_row = pl.multiple_of(half * rows_dev, 8)

    def quad_device(offset):
        place = lax.rem(quad + offset, nquad)
        return place, {"width": lax.div(place, nsub), "sub": lax.rem(place, nsub)}

    barrier = pltpu.get_barrier_semaphore()
    for j in range(1, ntok):
        pl.semaphore_signal(
            barrier, inc=1, device_id={"tok": lax.rem(mine + j, ntok)}, device_id_type=MESH
        )
    for i in range(1, nquad):
        pl.semaphore_signal(barrier, inc=1, device_id=quad_device(i)[1], device_id_type=MESH)

    loads = [
        pltpu.make_async_copy(
            sources[f], tokens.at[f, pl.ds(half_row, rows_dev), :], load_sem.at[f]
        )
        for f in range(2)
    ]
    for load in loads:
        load.start()

    line = lax.broadcasted_iota(jnp.int32, meta_out.shape, 0)
    lane = lax.broadcasted_iota(jnp.int32, meta_out.shape, 1)
    meta = jnp.zeros(meta_out.shape, jnp.int32)
    for a in range(local_q):
        here = lane == mine * local_q + a
        for k in range(topc):
            meta = jnp.where(here & (line == k), dest_ref[a, k], meta)
            meta = jnp.where(here & (line == topc + k), clus_ref[a, k], meta)
    meta_out[...] = meta
    meta_in[0] = meta

    def picked(target):
        seen = jnp.int32(0)
        found = [jnp.int32(0) for _ in range(CAP)]
        for a in range(local_q):
            named = dest_ref[a, 0] == target
            for k in range(1, topc):
                named = jnp.logical_or(named, dest_ref[a, k] == target)
            for e in range(CAP):
                found[e] = jnp.where(jnp.logical_and(named, seen == e), a, found[e])
            seen = seen + named.astype(jnp.int32)
        return found

    def pack(f):
        def one(j, carry):
            found = picked(lax.rem(mine + j, ntok))
            for e in range(CAP):
                outbox[f, j, e * rank : (e + 1) * rank, :] = factors[f][found[e]]
            return carry

        lax.fori_loop(1, ntok, one, 0)
        found = picked(mine)
        for e in range(CAP):
            inbox[f, 0, e * rank : (e + 1) * rank, :] = factors[f][found[e]]

    def fac_copy(f, c, j):
        cols = pl.ds(c * piece, piece)
        return pltpu.make_async_remote_copy(
            src_ref=outbox.at[f, j, :, cols],
            dst_ref=inbox.at[f, j, :, cols],
            send_sem=fac_send.at[f, c],
            recv_sem=fac_recv.at[f, c],
            device_id={"tok": lax.rem(mine + j, ntok)},
            device_id_type=MESH,
        )

    def fac_start(f, c):
        def one(j, carry):
            fac_copy(f, c, j).start()
            return carry

        lax.fori_loop(1, ntok, one, 0)

    def fac_all(f, c):
        cols = pl.ds(c * piece, piece)
        return pltpu.make_async_remote_copy(
            src_ref=outbox.at[f, pl.ds(1, ntok - 1), :, cols],
            dst_ref=inbox.at[f, pl.ds(1, ntok - 1), :, cols],
            send_sem=fac_send.at[f, c],
            recv_sem=fac_recv.at[f, c],
            device_id={"tok": lax.rem(mine + 1, ntok)},
            device_id_type=MESH,
        )

    def meta_copy(j):
        return pltpu.make_async_remote_copy(
            src_ref=meta_out,
            dst_ref=meta_in.at[j],
            send_sem=meta_send.at[j],
            recv_sem=meta_recv.at[j],
            device_id={"tok": lax.rem(mine + j, ntok)},
            device_id_type=MESH,
        )

    def tok_copy(f, i):
        return pltpu.make_async_remote_copy(
            src_ref=sources[f],
            dst_ref=tokens.at[f, pl.ds(half_row, rows_dev), :],
            send_sem=tok_send.at[f, i],
            recv_sem=tok_recv.at[f, i],
            device_id={"sub": lax.rem(half + i, nsub)},
            device_id_type=MESH,
        )

    def part_copy(f, i):
        place, device = quad_device(i)
        return pltpu.make_async_remote_copy(
            src_ref=acc.at[f, pl.ds(pl.multiple_of(place * share, 8), share), :],
            dst_ref=parts.at[f, i],
            send_sem=part_send.at[f, i],
            recv_sem=part_recv.at[f, i],
            device_id=device,
            device_id_type=MESH,
        )

    pack(0)
    pl.semaphore_wait(barrier, ntok - 1 + nquad - 1)
    for c in range(chunks):
        fac_start(0, c)
    for i in range(1, nsub):
        tok_copy(0, i).start()

    def meta_go(j, carry):
        meta_copy(j).start()
        return carry

    lax.fori_loop(1, ntok, meta_go, 0)
    for i in range(1, nsub):
        tok_copy(1, i).start()
    pack(1)

    step = 16

    def split(f, base):
        @pl.loop(0, rows_dev // step)
        def _(b):
            rows = pl.ds(pl.multiple_of(base + b * step, step), step)
            value = tokens[f, rows, :]
            top = value.astype(jnp.bfloat16)
            high[f, rows, :] = top
            low[f, rows, :] = (value - top.astype(jnp.float32)).astype(jnp.bfloat16)

    tile = 128

    def multiply(f, c):
        cols = pl.ds(c * piece, piece)

        @pl.loop(0, block_rows // tile)
        def _(b):
            rows = pl.ds(pl.multiple_of(b * tile, tile), tile)
            weight = inbox[f, :, :, cols].reshape(ntok * CAP * rank, piece)
            dims = (((1,), (1,)), ((), ()))
            value = lax.dot_general(
                high[f, rows, cols], weight, dims, preferred_element_type=jnp.float32
            ) + lax.dot_general(
                low[f, rows, cols], weight, dims, preferred_element_type=jnp.float32
            )
            if c == 0:
                acc[f, rows, :] = value
            else:
                acc[f, rows, :] += value

    for f in range(2):
        loads[f].wait()
        split(f, half * rows_dev)

    def meta_wait(j, carry):
        meta_copy(j).wait()
        return carry

    lax.fori_loop(1, ntok, meta_wait, 0)
    lists = jnp.sum(meta_in[...], axis=0)
    lane1 = lax.broadcasted_iota(jnp.int32, (8, lanes), 1)
    arrived = jnp.zeros((8, lanes), jnp.int32)
    label = jnp.zeros((8, lanes), jnp.int32)
    for k in range(topc):
        hit = (jnp.broadcast_to(lists[k : k + 1], (8, lanes)) == mine) & (lane1 < ntok * local_q)
        arrived = jnp.where(hit, 1, arrived)
        label = jnp.where(hit, jnp.broadcast_to(lists[topc + k : topc + k + 1], (8, lanes)), label)
    slot = jnp.zeros((8, lanes), jnp.int32)
    for a in range(1, local_q):
        slot = slot + jnp.where(
            lax.rem(lane1, local_q) >= a, pltpu.roll(arrived, a, axis=1), 0
        )
    width = ntok * CAP * rank
    place = lax.broadcasted_iota(jnp.int32, (width, lanes), 0)
    query = lax.broadcasted_iota(jnp.int32, (width, lanes), 1)
    origin = lax.rem(mine - lax.div(place, CAP * rank) + ntok, ntok)
    seat = lax.rem(lax.div(place, rank), CAP)
    chosen = (
        (arrived[0:1] == 1) & (slot[0:1] == seat) & (lax.div(query, local_q) == origin)
    )
    mapping = chosen.astype(jnp.float32)
    base = quad * share
    wide = tc_ref.shape[1]
    row = lax.broadcasted_iota(jnp.int32, (share, wide), 0) + base
    other = lax.broadcasted_iota(jnp.int32, (share, wide), 1)
    row_cluster = jnp.sum(
        jnp.where(row == other, tc_ref[...], 0).astype(jnp.float32), axis=1, keepdims=True
    )
    spot = lax.broadcasted_iota(jnp.int32, (share, lanes), 0) + base
    owner = lax.div(spot, rows_dev)
    limit = jnp.zeros((share, lanes), jnp.int32)
    for i in range(nsub):
        limit = jnp.where(owner == i, cnt_ref[mine * nsub + i], limit)
    live = (lax.rem(spot, rows_dev) < limit) & (row_cluster == label[0:1].astype(jnp.float32))
    live = live.astype(jnp.float32)

    for f in range(2):
        for i in range(1, nsub):
            tok_copy(f, i).wait()
            split(f, lax.rem(half + nsub - i, nsub) * rows_dev)
        for c in range(chunks):
            fac_all(f, c).wait_recv()
            if f == 0:
                fac_start(1, c)
            multiply(f, c)
        for i in range(1, nquad):
            part_copy(f, i).start()

    def total(f, h):
        start = pl.multiple_of(quad * share, 8)
        value = acc[f, pl.ds(start, share), :] if h == 0 else parts[f, h]
        for i in range(h + nsub, nquad, nsub):
            value = value + parts[f, i]
        return value

    for i in range(1, nquad):
        part_copy(0, i).wait_recv()
    for i in range(1, nquad):
        part_copy(1, i).wait_recv()
    product = total(0, 0) * total(1, 0)
    for h in range(1, nsub):
        product = product + total(0, h) * total(1, h)
    result = live * lax.dot_general(
        product,
        mapping,
        (((1,), (0,)), ((), ())),
        precision=lax.Precision.HIGHEST,
        preferred_element_type=jnp.float32,
    )
    out_ref[...] = result[:, : out_ref.shape[1]]

    for f in range(2):
        for c in range(chunks):
            fac_all(f, c).wait_send()
        for i in range(1, nquad):
            part_copy(f, i).wait_send()


def on_device(
    activation,
    cotangent,
    query_output_factor,
    query_input_factor,
    query_dest,
    query_cluster,
    token_cluster,
    token_count,
):
    ntok = lax.axis_size("tok")
    nsub = lax.axis_size("sub")
    nwide = lax.axis_size("width")
    local_q, topc = query_dest.shape
    rows_dev, depth = activation.shape
    rank = query_output_factor.shape[1]
    block_rows = rows_dev * nsub
    nquad = nwide * nsub
    share = block_rows // nquad
    lanes = -(-ntok * local_q // 128) * 128
    lines = -(-2 * topc // 8) * 8
    width = ntok * CAP * rank
    chunks = 4
    dma = pltpu.SemaphoreType.DMA
    vmem = pl.BlockSpec(memory_space=pltpu.VMEM)
    smem = pl.BlockSpec(memory_space=pltpu.SMEM)
    hbm = pl.BlockSpec(memory_space=pl.ANY)
    return pl.pallas_call(
        functools.partial(kernel, ntok, nwide, nsub, chunks),
        out_shape=jax.ShapeDtypeStruct((share, ntok * local_q), jnp.float32),
        in_specs=[hbm, hbm, vmem, vmem, smem, smem, vmem, smem],
        out_specs=vmem,
        scratch_shapes=[
            pltpu.VMEM((2, block_rows, depth), jnp.float32),
            pltpu.VMEM((2, block_rows, depth), jnp.bfloat16),
            pltpu.VMEM((2, block_rows, depth), jnp.bfloat16),
            pltpu.VMEM((2, ntok, CAP * rank, depth), jnp.bfloat16),
            pltpu.VMEM((2, ntok, CAP * rank, depth), jnp.bfloat16),
            pltpu.VMEM((2, block_rows, width), jnp.float32),
            pltpu.VMEM((2, nquad, share, width), jnp.float32),
            pltpu.VMEM((lines, lanes), jnp.int32),
            pltpu.VMEM((ntok, lines, lanes), jnp.int32),
            dma((2,)),
            dma((2, nsub)),
            dma((2, nsub)),
            dma((ntok,)),
            dma((ntok,)),
            dma((2, chunks)),
            dma((2, chunks)),
            dma((2, nquad)),
            dma((2, nquad)),
        ],
        compiler_params=pltpu.CompilerParams(
            collective_id=0, has_side_effects=True, vmem_limit_bytes=56 * 2**20
        ),
    )(
        activation,
        cotangent,
        query_output_factor,
        query_input_factor,
        query_dest,
        query_cluster,
        token_cluster.reshape(1, block_rows),
        token_count,
    )


def solution(mesh):
    placed = (
        P(("groups", "tok", "sub"), "width"),
        P(("groups", "tok", "sub"), "width"),
        P(("groups", "tok"), "sub", "width"),
        P(("groups", "tok"), "sub", "width"),
        P(("groups", "tok"), None),
        P(("groups", "tok"), None),
        P(("groups", "tok")),
        P("groups"),
    )
    return jax.shard_map(
        on_device,
        mesh=mesh,
        in_specs=placed,
        out_specs=P(("groups", "tok", "width", "sub"), None),
        check_vma=False,
    )
```

time: 113 us -> 65.1 us (0.58)
  Pallas kernels: 0 us -> 59.5 us
  waiting for transfers between devices: 28.9 us -> 0 us
  blocking collectives: 24.9 us -> 0 us
  matrix products: 16.1 us -> 0 us
  between operations: 13.9 us -> 0.01 us
  other arithmetic: 11.2 us -> 0 us
  starting transfers between devices: 11.2 us -> 0 us
    pallas_call x0 -> x1, Pallas kernels: none -> 59.5 us  [on_device(): pl.pallas_call(functools.partial(kernel, ntok, nwide, nsub, chunks), out_...]
    unnamed x1 -> x0, blocking collectives: 24.9 us -> none
    unnamed x6 -> x0, waiting for transfers between devices: 16.8 us -> none
    dot_general x5 -> x0, matrix products: 15.2 us -> none  [the longest x1 5.87 us: on_device(): jnp.einsum('tk,nmrk->tmnr', acts_all, got_v, precision=lax.Precision.HIGH...]
    all_to_all x2 -> x0, waiting for transfers between devices: 12 us -> none  [the longest x1 12 us: on_device(): lax.all_to_all(send_v, 'tok', split_axis=0, concat_axis=0, tiled=True)]
    all_to_all x2 -> x0, starting transfers between devices: 10.3 us -> none  [the longest x1 6.02 us: on_device(): lax.all_to_all(send_u, 'tok', split_axis=0, concat_axis=0, tiled=True)]
    select_n x2 -> x0, other arithmetic: 8.44 us -> none  [the longest x1 5.15 us: on_device(): jnp.where(first, activation, other_act)]
    unnamed x22 -> x2, local copies, waits for them, and re-layouts: 5.86 us -> 2.62 us
  transfers between devices with their start and end apart: 7 -> 0, of which waited for: 3 -> 0; matrix products, arithmetic and copies ran while one was open for 26% -> 0% of each run, Pallas kernels for 0% -> 0%
where the time goes in v1:
time: 65.1 us; the launch traced here: 64.8 us
  Pallas kernels  59.5 us (91%)
  local copies, waits for them, and re-layouts  5.31 us (8%)
    pallas_call x1, Pallas kernels, on_device(): pl.pallas_call(functools.partial(kernel, ntok, nwide, nsub, chunks), out_...  59.5 us
    unnamed x2, local copies, waits for them, and re-layouts  2.62 us
    pallas_call x1, local copies, waits for them, and re-layouts, on_device(): pl.pallas_call(functools.partial(kernel, ntok, nwide, nsub, chunks), out_...  1.47 us

profile of v1, /device:TPU:0, one launch (start us, length us, event | category | flops | bytes accessed | tf_op | source)
XLA Modules:
  0.0 64.8 jit_solution(13263734209188820225)
XLA Ops:
  0.0 1.2 %reshape.3.tc_ref = s32[1,384]{1,0:T(1,128)} reshape(s32[384]{0:T(512)} %param.14) | data formatting | bytes 3072 | tf_op jit(solution)/shard_map/reshape | solution.py:376
  1.2 1.3 %copy.9.dest_ref = s32[4,1]{1,0:T(4,128)} copy(s32[4,1]{0,1:T(1,128)} %param.12) | data formatting | bytes 32 | tf_op args[4]
  2.5 1.3 %copy.10.clus_ref = s32[4,1]{1,0:T(4,128)} copy(s32[4,1]{0,1:T(1,128)} %param.13) | data formatting | bytes 32 | tf_op args[5]
  3.8 59.5 %shard_map.82 = f32[96,16]{1,0:T(8,128)} custom-call(f32[192,4096]{1,0:T(8,128)} %act_hbm.1, f32[192,4096]{1,0:T(8,128)} %cot_hbm.1, bf16[4,16,4096]{2,1,0:T(8,128)(2,1)} %u_ref.1, bf16[4,16,4096]{2,1,0:T(8,128)(2,1)} %v_ref.1, s32[4,1]{1,0:T(4,128)} %copy.9.dest_ref, s32[4,1]{1,0:T(4,128)} %copy.10.clus_ref, s32[1,384]{1,0:T(1,128)} %reshape.3.tc_ref, s32[8]{0:T(128)} %cnt_ref.1), custom_call_target="tpu_custom_call" | custom-call | tf_op jit(solution)/shard_map/pallas_call | solution.py:341
  63.4 1.5 %copy.11 = f32[96,16]{0,1:T(8,128)} copy(f32[96,16]{1,0:T(8,128)} %shard_map.82) | data formatting | bytes 12288 | tf_op jit(solution)/shard_map/pallas_call | solution.py:341

commit v2 on v1

--- a/solution.py
+++ b/solution.py
@@ -11,17 +11,97 @@
 MESH = pl.DeviceIdType.MESH
 
 
+def over_lanes(lists, topc, local_q, count):
+    shape = (8, lists.shape[1])
+    lane = lax.broadcasted_iota(jnp.int32, shape, 1)
+    named = [jnp.broadcast_to(lists[k : k + 1], shape) for k in range(topc)]
+    total = jnp.zeros(shape, jnp.int32)
+    for k in range(topc):
+        again = jnp.zeros(shape, jnp.int32)
+        for a in range(1, local_q):
+            earlier = (lax.rem(lane, local_q) >= a) & (lane < count)
+            for other in range(topc):
+                same = named[k] == pltpu.roll(named[other], a, axis=1)
+                again = jnp.where(earlier & same, 1, again)
+        total = total + again
+    return total
+
+
+def meta_kernel(
+    ngroup, ntok, dest_ref, clus_ref, lists_ref, count_ref, meta_out, meta_in, send, recv
+):
+    group = lax.axis_index("groups")
+    mine = lax.axis_index("tok")
+    topc, local_q = dest_ref.shape
+    everyone = ngroup * ntok
+
+    def device(p):
+        return {
+            "groups": lax.rem(group + lax.div(p, ntok), ngroup),
+            "tok": lax.rem(mine + lax.rem(p, ntok), ntok),
+        }
+
+    barrier = pltpu.get_barrier_semaphore()
+
+    def greet(p, carry):
+        pl.semaphore_signal(barrier, inc=1, device_id=device(p), device_id_type=MESH)
+        return carry
+
+    lax.fori_loop(1, everyone, greet, 0)
+    line = lax.broadcasted_iota(jnp.int32, meta_out.shape, 0)
+    lane = lax.broadcasted_iota(jnp.int32, meta_out.shape, 1)
+    meta = jnp.zeros(meta_out.shape, jnp.int32)
+    for a in range(local_q):
+        here = lane == mine * local_q + a
+        for k in range(topc):
+            meta = jnp.where(here & (line == k), dest_ref[k, a], meta)
+            meta = jnp.where(here & (line == topc + k), clus_ref[k, a], meta)
+    meta_out[...] = meta
+    meta_in[0] = meta
+    pl.semaphore_wait(barrier, everyone - 1)
+
+    def copy(p):
+        return pltpu.make_async_remote_copy(
+            src_ref=meta_out,
+            dst_ref=meta_in.at[p],
+            send_sem=send.at[p],
+            recv_sem=recv.at[p],
+            device_id=device(p),
+            device_id_type=MESH,
+        )
+
+    def go(p, carry):
+        copy(p).start()
+        return carry
+
+    def done(p, carry):
+        copy(p).wait()
+        return carry
+
+    lax.fori_loop(1, everyone, go, 0)
+    lax.fori_loop(1, everyone, done, 0)
+    most = jnp.float32(0)
+    for g in range(ngroup):
+        lists = jnp.sum(meta_in[g * ntok : (g + 1) * ntok], axis=0)
+        if g == 0:
+            lists_ref[...] = lists
+        over = over_lanes(lists, topc, local_q, ntok * local_q)
+        most = jnp.maximum(most, jnp.sum(over[0:1].astype(jnp.float32)))
+    count_ref[0] = most.astype(jnp.int32)
+
+
 def kernel(
     ntok,
     nwide,
     nsub,
     chunks,
+    lean,
     act_hbm,
     cot_hbm,
     u_ref,
     v_ref,
     dest_ref,
-    clus_ref,
+    lists_ref,
     tc_ref,
     cnt_ref,
     out_ref,
@@ -32,13 +112,12 @@
     inbox,
     acc,
     parts,
-    meta_out,
-    meta_in,
+    relay,
     load_sem,
     tok_send,
     tok_recv,
-    meta_send,
-    meta_recv,
+    relay_send,
+    relay_recv,
     fac_send,
     fac_recv,
     part_send,
@@ -47,11 +126,13 @@
     mine = lax.axis_index("tok")
     column = lax.axis_index("width")
     half = lax.axis_index("sub")
-    local_q, topc = dest_ref.shape
+    topc, local_q = dest_ref.shape
     rows_dev, depth = act_hbm.shape
     block_rows = rows_dev * nsub
     rank = u_ref.shape[1]
-    lanes = meta_out.shape[1]
+    lanes = lists_ref.shape[1]
+    seats = 1 if lean else CAP
+    places = inbox.shape[1]
     piece = depth // chunks
     nquad = nwide * nsub
     quad = column * nsub + half
@@ -81,40 +162,81 @@
     for load in loads:
         load.start()
 
-    line = lax.broadcasted_iota(jnp.int32, meta_out.shape, 0)
-    lane = lax.broadcasted_iota(jnp.int32, meta_out.shape, 1)
-    meta = jnp.zeros(meta_out.shape, jnp.int32)
-    for a in range(local_q):
-        here = lane == mine * local_q + a
-        for k in range(topc):
-            meta = jnp.where(here & (line == k), dest_ref[a, k], meta)
-            meta = jnp.where(here & (line == topc + k), clus_ref[a, k], meta)
-    meta_out[...] = meta
-    meta_in[0] = meta
-
     def picked(target):
         seen = jnp.int32(0)
         found = [jnp.int32(0) for _ in range(CAP)]
         for a in range(local_q):
-            named = dest_ref[a, 0] == target
+            named = dest_ref[0, a] == target
             for k in range(1, topc):
-                named = jnp.logical_or(named, dest_ref[a, k] == target)
+                named = jnp.logical_or(named, dest_ref[k, a] == target)
             for e in range(CAP):
                 found[e] = jnp.where(jnp.logical_and(named, seen == e), a, found[e])
             seen = seen + named.astype(jnp.int32)
         return found
 
+    extra = jnp.int32(0)
+    holds = jnp.int32(0)
+    for a in range(1, local_q):
+        for before in range(a):
+            for k in range(topc):
+                for other in range(topc):
+                    same = dest_ref[k, a] == dest_ref[other, before]
+                    extra = jnp.where(same, a, extra)
+                    holds = jnp.where(same, 1, holds)
+
+    def relay_copy(f, c, way):
+        cols = pl.ds(c * piece, piece)
+        step = 1 if way == 0 else ntok - 1
+        return pltpu.make_async_remote_copy(
+            src_ref=relay.at[way, f, :, cols],
+            dst_ref=inbox.at[f, ntok + way, :, cols],
+            send_sem=relay_send.at[way, f, c],
+            recv_sem=relay_recv.at[way, f, c],
+            device_id={"tok": lax.rem(mine + step, ntok)},
+            device_id_type=MESH,
+        )
+
+    first, last = mine == 0, mine == ntok - 1
+
+    def forward(f, c):
+        cols = pl.ds(c * piece, piece)
+        for way in range(2):
+            starts, ends = (first, last) if way == 0 else (last, first)
+
+            @pl.when(jnp.logical_not(starts))
+            def _():
+                relay_copy(f, c, way).wait_recv()
+
+            @pl.when(jnp.logical_not(ends))
+            def _():
+                relay[way, f, :, cols] = jnp.where(
+                    holds == 1, inbox[f, ntok + 2, :, cols], inbox[f, ntok + way, :, cols]
+                )
+                relay_copy(f, c, way).start()
+
     def pack(f):
         def one(j, carry):
             found = picked(lax.rem(mine + j, ntok))
-            for e in range(CAP):
+            for e in range(seats):
                 outbox[f, j, e * rank : (e + 1) * rank, :] = factors[f][found[e]]
             return carry
 
         lax.fori_loop(1, ntok, one, 0)
         found = picked(mine)
-        for e in range(CAP):
+        for e in range(seats):
             inbox[f, 0, e * rank : (e + 1) * rank, :] = factors[f][found[e]]
+        if lean:
+            value = factors[f][extra]
+            inbox[f, ntok + 2] = value
+            inbox[f, ntok + 3] = value
+
+            @pl.when(mine == 0)
+            def _():
+                inbox[f, ntok] = jnp.zeros_like(value)
+
+            @pl.when(mine == ntok - 1)
+            def _():
+                inbox[f, ntok + 1] = jnp.zeros_like(value)
 
     def fac_copy(f, c, j):
         cols = pl.ds(c * piece, piece)
@@ -145,16 +267,6 @@
             device_id_type=MESH,
         )
 
-    def meta_copy(j):
-        return pltpu.make_async_remote_copy(
-            src_ref=meta_out,
-            dst_ref=meta_in.at[j],
-            send_sem=meta_send.at[j],
-            recv_sem=meta_recv.at[j],
-            device_id={"tok": lax.rem(mine + j, ntok)},
-            device_id_type=MESH,
-        )
-
     def tok_copy(f, i):
         return pltpu.make_async_remote_copy(
             src_ref=sources[f],
@@ -176,18 +288,15 @@
             device_id_type=MESH,
         )
 
+    pieces = [(f, c) for f in range(2) for c in range(chunks)]
+    ahead = 4
+    lag = 3 if lean else 0
     pack(0)
     pl.semaphore_wait(barrier, ntok - 1 + nquad - 1)
-    for c in range(chunks):
-        fac_start(0, c)
+    for f, c in pieces[:ahead]:
+        fac_start(f, c)
     for i in range(1, nsub):
         tok_copy(0, i).start()
-
-    def meta_go(j, carry):
-        meta_copy(j).start()
-        return carry
-
-    lax.fori_loop(1, ntok, meta_go, 0)
     for i in range(1, nsub):
         tok_copy(1, i).start()
     pack(1)
@@ -211,7 +320,7 @@
         @pl.loop(0, block_rows // tile)
         def _(b):
             rows = pl.ds(pl.multiple_of(b * tile, tile), tile)
-            weight = inbox[f, :, :, cols].reshape(ntok * CAP * rank, piece)
+            weight = inbox[f, :, :, cols].reshape(places * seats * rank, piece)
             dims = (((1,), (1,)), ((), ()))
             value = lax.dot_general(
                 high[f, rows, cols], weight, dims, preferred_element_type=jnp.float32
@@ -223,16 +332,15 @@
             else:
                 acc[f, rows, :] += value
 
+    if lean:
+        forward(*pieces[0])
     for f in range(2):
         loads[f].wait()
         split(f, half * rows_dev)
-
-    def meta_wait(j, carry):
-        meta_copy(j).wait()
-        return carry
-
-    lax.fori_loop(1, ntok, meta_wait, 0)
-    lists = jnp.sum(meta_in[...], axis=0)
+        if lean:
+            forward(*pieces[1 + f])
+
+    lists = lists_ref[...]
     lane1 = lax.broadcasted_iota(jnp.int32, (8, lanes), 1)
     arrived = jnp.zeros((8, lanes), jnp.int32)
     label = jnp.zeros((8, lanes), jnp.int32)
@@ -245,21 +353,29 @@
         slot = slot + jnp.where(
             lax.rem(lane1, local_q) >= a, pltpu.roll(arrived, a, axis=1), 0
         )
-    width = ntok * CAP * rank
+    width = places * seats * rank
     place = lax.broadcasted_iota(jnp.int32, (width, lanes), 0)
     query = lax.broadcasted_iota(jnp.int32, (width, lanes), 1)
-    origin = lax.rem(mine - lax.div(place, CAP * rank) + ntok, ntok)
-    seat = lax.rem(lax.div(place, rank), CAP)
-    chosen = (
-        (arrived[0:1] == 1) & (slot[0:1] == seat) & (lax.div(query, local_q) == origin)
-    )
+    spot = lax.div(place, seats * rank)
+    origin = lax.rem(mine - spot + 2 * ntok, ntok)
+    source = lax.div(query, local_q)
+    seat = lax.rem(lax.div(place, rank), seats)
+    chosen = (slot[0:1] == seat) & (source == origin) & (spot < ntok)
+    if lean:
+        passed = (
+            ((spot == ntok) & (source < mine))
+            | ((spot == ntok + 1) & (source > mine))
+            | ((spot == ntok + 2) & (source == mine))
+        )
+        chosen = chosen | ((slot[0:1] == 1) & passed)
+    chosen = (arrived[0:1] == 1) & chosen
     mapping = chosen.astype(jnp.float32)
     base = quad * share
-    wide = tc_ref.shape[1]
+    wide = tc_ref.shape[0]
     row = lax.broadcasted_iota(jnp.int32, (share, wide), 0) + base
     other = lax.broadcasted_iota(jnp.int32, (share, wide), 1)
     row_cluster = jnp.sum(
-        jnp.where(row == other, tc_ref[...], 0).astype(jnp.float32), axis=1, keepdims=True
+        jnp.where(row == other, tc_ref[...].reshape(1, wide), 0).astype(jnp.float32), axis=1, keepdims=True
     )
     spot = lax.broadcasted_iota(jnp.int32, (share, lanes), 0) + base
     owner = lax.div(spot, rows_dev)
@@ -269,17 +385,20 @@
     live = (lax.rem(spot, rows_dev) < limit) & (row_cluster == label[0:1].astype(jnp.float32))
     live = live.astype(jnp.float32)
 
-    for f in range(2):
-        for i in range(1, nsub):
-            tok_copy(f, i).wait()
-            split(f, lax.rem(half + nsub - i, nsub) * rows_dev)
-        for c in range(chunks):
-            fac_all(f, c).wait_recv()
-            if f == 0:
-                fac_start(1, c)
-            multiply(f, c)
-        for i in range(1, nquad):
-            part_copy(f, i).start()
+    for p, (f, c) in enumerate(pieces):
+        if lean and p + lag < len(pieces):
+            forward(*pieces[p + lag])
+        if c == 0:
+            for i in range(1, nsub):
+                tok_copy(f, i).wait()
+                split(f, lax.rem(half + nsub - i, nsub) * rows_dev)
+        fac_all(f, c).wait_recv()
+        if p + ahead < len(pieces):
+            fac_start(*pieces[p + ahead])
+        multiply(f, c)
+        if c == chunks - 1:
+            for i in range(1, nquad):
+                part_copy(f, i).start()
 
     def total(f, h):
         start = pl.multiple_of(quad * share, 8)
@@ -302,13 +421,20 @@
         precision=lax.Precision.HIGHEST,
         preferred_element_type=jnp.float32,
     )
-    out_ref[...] = result[:, : out_ref.shape[1]]
+    out_ref[...] = result.T[: out_ref.shape[0], :]
 
     for f in range(2):
         for c in range(chunks):
             fac_all(f, c).wait_send()
         for i in range(1, nquad):
             part_copy(f, i).wait_send()
+    if lean:
+        for f, c in pieces:
+            for way, ends in ((0, last), (1, first)):
+
+                @pl.when(jnp.logical_not(ends))
+                def _():
+                    relay_copy(f, c, way).wait_send()
 
 
 def on_device(
@@ -332,50 +458,79 @@
     share = block_rows // nquad
     lanes = -(-ntok * local_q // 128) * 128
     lines = -(-2 * topc // 8) * 8
-    width = ntok * CAP * rank
+    ngroup = lax.axis_size("groups")
     chunks = 4
     dma = pltpu.SemaphoreType.DMA
     vmem = pl.BlockSpec(memory_space=pltpu.VMEM)
     smem = pl.BlockSpec(memory_space=pltpu.SMEM)
     hbm = pl.BlockSpec(memory_space=pl.ANY)
-    return pl.pallas_call(
-        functools.partial(kernel, ntok, nwide, nsub, chunks),
-        out_shape=jax.ShapeDtypeStruct((share, ntok * local_q), jnp.float32),
-        in_specs=[hbm, hbm, vmem, vmem, smem, smem, vmem, smem],
-        out_specs=vmem,
+    dest, clus = query_dest.T, query_cluster.T
+    lists, count = pl.pallas_call(
+        functools.partial(meta_kernel, ngroup, ntok),
+        out_shape=(
+            jax.ShapeDtypeStruct((lines, lanes), jnp.int32),
+            jax.ShapeDtypeStruct((1,), jnp.int32),
+        ),
+        in_specs=[smem, smem],
+        out_specs=(vmem, smem),
         scratch_shapes=[
-            pltpu.VMEM((2, block_rows, depth), jnp.float32),
-            pltpu.VMEM((2, block_rows, depth), jnp.bfloat16),
-            pltpu.VMEM((2, block_rows, depth), jnp.bfloat16),
-            pltpu.VMEM((2, ntok, CAP * rank, depth), jnp.bfloat16),
-            pltpu.VMEM((2, ntok, CAP * rank, depth), jnp.bfloat16),
-            pltpu.VMEM((2, block_rows, width), jnp.float32),
-            pltpu.VMEM((2, nquad, share, width), jnp.float32),
             pltpu.VMEM((lines, lanes), jnp.int32),
-            pltpu.VMEM((ntok, lines, lanes), jnp.int32),
-            dma((2,)),
-            dma((2, nsub)),
-            dma((2, nsub)),
-            dma((ntok,)),
-            dma((ntok,)),
-            dma((2, chunks)),
-            dma((2, chunks)),
-            dma((2, nquad)),
-            dma((2, nquad)),
+            pltpu.VMEM((ngroup * ntok, lines, lanes), jnp.int32),
+            dma((ngroup * ntok,)),
+            dma((ngroup * ntok,)),
         ],
-        compiler_params=pltpu.CompilerParams(
-            collective_id=0, has_side_effects=True, vmem_limit_bytes=56 * 2**20
-        ),
-    )(
+        compiler_params=pltpu.CompilerParams(collective_id=0, has_side_effects=True),
+    )(dest, clus)
+
+    def call(lean, *args):
+        seats = 1 if lean else CAP
+        places = ntok + 4 if lean else ntok
+        width = places * seats * rank
+        return pl.pallas_call(
+            functools.partial(kernel, ntok, nwide, nsub, chunks, lean),
+            out_shape=jax.ShapeDtypeStruct((ntok * local_q, share), jnp.float32),
+            in_specs=[hbm, hbm, vmem, vmem, smem, vmem, vmem, smem],
+            out_specs=vmem,
+            scratch_shapes=[
+                pltpu.VMEM((2, block_rows, depth), jnp.float32),
+                pltpu.VMEM((2, block_rows, depth), jnp.bfloat16),
+                pltpu.VMEM((2, block_rows, depth), jnp.bfloat16),
+                pltpu.VMEM((2, ntok, seats * rank, depth), jnp.bfloat16),
+                pltpu.VMEM((2, places, seats * rank, depth), jnp.bfloat16),
+                pltpu.VMEM((2, block_rows, width), jnp.float32),
+                pltpu.VMEM((2, nquad, share, width), jnp.float32),
+                pltpu.VMEM((2, 2, rank, depth), jnp.bfloat16),
+                dma((2,)),
+                dma((2, nsub)),
+                dma((2, nsub)),
+                dma((2, 2, chunks)),
+                dma((2, 2, chunks)),
+                dma((2, chunks)),
+                dma((2, chunks)),
+                dma((2, nquad)),
+                dma((2, nquad)),
+            ],
+            compiler_params=pltpu.CompilerParams(
+                collective_id=1 if lean else 2,
+                has_side_effects=True,
+                vmem_limit_bytes=56 * 2**20,
+            ),
+        )(*args)
+
+    scores = lax.cond(
+        count[0] <= 1,
+        functools.partial(call, True),
+        functools.partial(call, False),
         activation,
         cotangent,
         query_output_factor,
         query_input_factor,
-        query_dest,
-        query_cluster,
-        token_cluster.reshape(1, block_rows),
+        dest,
+        lists,
+        token_cluster,
         token_count,
     )
+    return scores.T
 
 
 def solution(mesh):

time: 65.1 us -> 179 us (2.75)
  Pallas kernels: 59.5 us -> 178 us
  local copies, waits for them, and re-layouts: 5.31 us -> 0.6 us
    pallas_call x1 -> x2, Pallas kernels: 59.5 us -> 178 us  [the longest x1 168 us: call(): pl.pallas_call(functools.partial(kernel, ntok, nwide, nsub, chunks, lean)...]
    unnamed x2 -> x1, local copies, waits for them, and re-layouts: 2.62 us -> 0.6 us
where the time goes in v2:
time: 179 us
  Pallas kernels  178 us (99%)
    pallas_call x1, Pallas kernels, call(): pl.pallas_call(functools.partial(kernel, ntok, nwide, nsub, chunks, lean)...  168 us
    pallas_call x1, Pallas kernels, on_device(): pl.pallas_call(functools.partial(meta_kernel, ngroup, ntok), out_shape=(j...  9.99 us

profile of v2, /device:TPU:0, one launch (start us, length us, event | category | flops | bytes accessed | tf_op | source)
XLA Modules:
  0.0 179.0 jit_solution(10957731209227510071)
XLA Ops:
  0.0 10.0 %shard_map.82 = (s32[8,128]{1,0:T(8,128)S(1)}, s32[1]{0:T(128)}) custom-call(s32[1,4]{1,0:T(1,128)} %bitcast.5, s32[1,4]{1,0:T(1,128)} %bitcast.8), custom_call_target="tpu_custom_call" | custom-call | tf_op jit(solution)/shard_map/pallas_call | solution.py:468
  10.6 167.7 %conditional.1 = (f32[16,96]{1,0:T(8,128)S(1)}) conditional(s32[]{:T(128)} %bitcast.2, (f32[192,4096]{1,0:T(8,128)}, f32[192,4096]{1,0:T(8,128)}, bf16[4,16,4096]{2,1,0:T(8,128)(2,1)}, bf16[4,16,4096]{2,1,0:T(8,128)(2,1)}, s32[1,4]{1,0:T(1,128)}, /*index=5*/s32[8,128]{1,0:T(8,128)S(1)}, s32[384]{0:T(512)}, s32[8]{0:T(128)}) %tuple.14, ...), branch_computations={%region_0.0_spmd, %region_1.0_spmd} | conditional | bytes 8 | solution.py:520
  10.6 167.7 %branch_1_fun.1 = f32[16,96]{1,0:T(8,128)S(1)} custom-call(f32[192,4096]{1,0:T(8,128)} %get-tuple-element.48.act_hbm, f32[192,4096]{1,0:T(8,128)} %get-tuple-element.49.cot_hbm, bf16[4,16,4096]{2,1,0:T(8,128)(2,1)} %get-tuple-element.50.u_ref, bf16[4,16,4096]{2,1,0:T(8,128)(2,1)} %get-tuple-element.51.v_ref, s32[1,4]{1,0:T(1,128)} %get-tuple-element.52.dest_ref, ...), custom_call_target="tpu_custom_call" | custom-call | tf_op jit(solution)/shard_map/cond/branch_1_fun/pallas_call | solution.py:489
  178.4 0.6 copy.12

commit v3 on v1

--- a/solution.py
+++ b/solution.py
@@ -47,7 +47,7 @@
     mine = lax.axis_index("tok")
     column = lax.axis_index("width")
     half = lax.axis_index("sub")
-    local_q, topc = dest_ref.shape
+    topc, local_q = dest_ref.shape
     rows_dev, depth = act_hbm.shape
     block_rows = rows_dev * nsub
     rank = u_ref.shape[1]
@@ -87,8 +87,8 @@
     for a in range(local_q):
         here = lane == mine * local_q + a
         for k in range(topc):
-            meta = jnp.where(here & (line == k), dest_ref[a, k], meta)
-            meta = jnp.where(here & (line == topc + k), clus_ref[a, k], meta)
+            meta = jnp.where(here & (line == k), dest_ref[k, a], meta)
+            meta = jnp.where(here & (line == topc + k), clus_ref[k, a], meta)
     meta_out[...] = meta
     meta_in[0] = meta
 
@@ -96,9 +96,9 @@
         seen = jnp.int32(0)
         found = [jnp.int32(0) for _ in range(CAP)]
         for a in range(local_q):
-            named = dest_ref[a, 0] == target
+            named = dest_ref[0, a] == target
             for k in range(1, topc):
-                named = jnp.logical_or(named, dest_ref[a, k] == target)
+                named = jnp.logical_or(named, dest_ref[k, a] == target)
             for e in range(CAP):
                 found[e] = jnp.where(jnp.logical_and(named, seen == e), a, found[e])
             seen = seen + named.astype(jnp.int32)
@@ -255,11 +255,11 @@
     )
     mapping = chosen.astype(jnp.float32)
     base = quad * share
-    wide = tc_ref.shape[1]
+    wide = tc_ref.shape[0]
     row = lax.broadcasted_iota(jnp.int32, (share, wide), 0) + base
     other = lax.broadcasted_iota(jnp.int32, (share, wide), 1)
     row_cluster = jnp.sum(
-        jnp.where(row == other, tc_ref[...], 0).astype(jnp.float32), axis=1, keepdims=True
+        jnp.where(row == other, tc_ref[...].reshape(1, wide), 0).astype(jnp.float32), axis=1, keepdims=True
     )
     spot = lax.broadcasted_iota(jnp.int32, (share, lanes), 0) + base
     owner = lax.div(spot, rows_dev)
@@ -302,7 +302,7 @@
         precision=lax.Precision.HIGHEST,
         preferred_element_type=jnp.float32,
     )
-    out_ref[...] = result[:, : out_ref.shape[1]]
+    out_ref[...] = result.T[: out_ref.shape[0], :]
 
     for f in range(2):
         for c in range(chunks):
@@ -333,14 +333,14 @@
     lanes = -(-ntok * local_q // 128) * 128
     lines = -(-2 * topc // 8) * 8
     width = ntok * CAP * rank
-    chunks = 4
+    chunks = 2
     dma = pltpu.SemaphoreType.DMA
     vmem = pl.BlockSpec(memory_space=pltpu.VMEM)
     smem = pl.BlockSpec(memory_space=pltpu.SMEM)
     hbm = pl.BlockSpec(memory_space=pl.ANY)
     return pl.pallas_call(
         functools.partial(kernel, ntok, nwide, nsub, chunks),
-        out_shape=jax.ShapeDtypeStruct((share, ntok * local_q), jnp.float32),
+        out_shape=jax.ShapeDtypeStruct((ntok * local_q, share), jnp.float32),
         in_specs=[hbm, hbm, vmem, vmem, smem, smem, vmem, smem],
         out_specs=vmem,
         scratch_shapes=[
@@ -371,11 +371,11 @@
         cotangent,
         query_output_factor,
         query_input_factor,
-        query_dest,
-        query_cluster,
-        token_cluster.reshape(1, block_rows),
+        query_dest.T,
+        query_cluster.T,
+        token_cluster,
         token_count,
-    )
+    ).T
 
 
 def solution(mesh):

time: 65.1 us -> 60.5 us (0.929)
  local copies, waits for them, and re-layouts: 5.31 us -> 1.3 us
    pallas_call x1 -> x0, local copies, waits for them, and re-layouts: 1.47 us -> none  [on_device(): pl.pallas_call(functools.partial(kernel, ntok, nwide, nsub, chunks), out_...]
    unnamed x2 -> x1, local copies, waits for them, and re-layouts: 2.62 us -> 1.3 us
    reshape x1 -> x0, local copies, waits for them, and re-layouts: 1.22 us -> none  [on_device(): token_cluster.reshape(1, block_rows)]
where the time goes in v3:
time: 60.5 us; the launch traced here: 60.2 us
  Pallas kernels  58.9 us (97%)
  local copies, waits for them, and re-layouts  1.3 us (2%)
    pallas_call x1, Pallas kernels, on_device(): pl.pallas_call(functools.partial(kernel, ntok, nwide, nsub, chunks), out_...  58.9 us
    unnamed x1, local copies, waits for them, and re-layouts  1.3 us

profile of v3, /device:TPU:0, one launch (start us, length us, event | category | flops | bytes accessed | tf_op | source)
XLA Modules:
  0.0 60.2 jit_solution(18063921882193463389)
XLA Ops:
  0.0 58.9 %shard_map.82 = f32[16,96]{1,0:T(8,128)} custom-call(f32[192,4096]{1,0:T(8,128)} %act_hbm.1, f32[192,4096]{1,0:T(8,128)} %cot_hbm.1, bf16[4,16,4096]{2,1,0:T(8,128)(2,1)} %u_ref.1, bf16[4,16,4096]{2,1,0:T(8,128)(2,1)} %v_ref.1, s32[1,4]{1,0:T(1,128)} %bitcast.4, s32[1,4]{1,0:T(1,128)} %bitcast.5, s32[384]{0:T(512)} %tc_ref.1, s32[8]{0:T(128)} %cnt_ref.1), custom_call_target="tpu_custom_call" | custom-call | tf_op jit(solution)/shard_map/pallas_call | solution.py:341
  58.9 1.3 %copy.10 = f32[96,16]{0,1:T(8,128)} copy(f32[96,16]{0,1:T(8,128)} %bitcast.3) | data formatting | bytes 12288

commit v4 on v2

--- a/solution.py
+++ b/solution.py
@@ -8,6 +8,8 @@
 from jax.sharding import PartitionSpec as P
 
 CAP = 2
+CHUNKS = 4
+AHEAD = 3
 MESH = pl.DeviceIdType.MESH
 
 
@@ -145,6 +147,7 @@
         place = lax.rem(quad + offset, nquad)
         return place, {"width": lax.div(place, nsub), "sub": lax.rem(place, nsub)}
 
+    pieces = [(f, c) for f in range(2) for c in range(chunks)]
     barrier = pltpu.get_barrier_semaphore()
     for j in range(1, ntok):
         pl.semaphore_signal(
@@ -198,21 +201,47 @@
 
     first, last = mine == 0, mine == ntok - 1
 
-    def forward(f, c):
+    def relay_send_on(f, c, way, starts):
         cols = pl.ds(c * piece, piece)
+        mask = holds == 1
+        if starts:
+            relay[way, f, :, cols] = inbox[f, ntok + 2, :, cols]
+        else:
+            relay_copy(f, c, way).wait_recv()
+            relay[way, f, :, cols] = jnp.where(
+                mask, inbox[f, ntok + 2, :, cols], inbox[f, ntok + way, :, cols]
+            )
+        relay_copy(f, c, way).start()
+
+    def begin(f, c):
+        @pl.when(first)
+        def _():
+            relay_send_on(f, c, 0, True)
+
+        @pl.when(last)
+        def _():
+            relay_send_on(f, c, 1, True)
+
+    inner = jnp.logical_not(jnp.logical_or(first, last))
+    lower = mine < ntok // 2
+
+    def forward(turn):
         for way in range(2):
-            starts, ends = (first, last) if way == 0 else (last, first)
-
-            @pl.when(jnp.logical_not(starts))
+            near = lower if way == turn else jnp.logical_not(lower)
+
+            @pl.when(jnp.logical_and(inner, near))
             def _():
-                relay_copy(f, c, way).wait_recv()
-
-            @pl.when(jnp.logical_not(ends))
-            def _():
-                relay[way, f, :, cols] = jnp.where(
-                    holds == 1, inbox[f, ntok + 2, :, cols], inbox[f, ntok + way, :, cols]
-                )
-                relay_copy(f, c, way).start()
+                for f, c in pieces:
+                    relay_send_on(f, c, way, False)
+
+    def arrive(f, c):
+        @pl.when(last)
+        def _():
+            relay_copy(f, c, 0).wait_recv()
+
+        @pl.when(first)
+        def _():
+            relay_copy(f, c, 1).wait_recv()
 
     def pack(f):
         def one(j, carry):
@@ -288,18 +317,21 @@
             device_id_type=MESH,
         )
 
-    pieces = [(f, c) for f in range(2) for c in range(chunks)]
-    ahead = 4
-    lag = 3 if lean else 0
+    ahead = AHEAD
     pack(0)
+    pack(1)
     pl.semaphore_wait(barrier, ntok - 1 + nquad - 1)
+    if lean:
+        for f, c in pieces:
+            begin(f, c)
+        forward(0)
+        forward(1)
     for f, c in pieces[:ahead]:
         fac_start(f, c)
     for i in range(1, nsub):
         tok_copy(0, i).start()
     for i in range(1, nsub):
         tok_copy(1, i).start()
-    pack(1)
 
     step = 16
 
@@ -332,13 +364,9 @@
             else:
                 acc[f, rows, :] += value
 
-    if lean:
-        forward(*pieces[0])
     for f in range(2):
         loads[f].wait()
         split(f, half * rows_dev)
-        if lean:
-            forward(*pieces[1 + f])
 
     lists = lists_ref[...]
     lane1 = lax.broadcasted_iota(jnp.int32, (8, lanes), 1)
@@ -386,15 +414,15 @@
     live = live.astype(jnp.float32)
 
     for p, (f, c) in enumerate(pieces):
-        if lean and p + lag < len(pieces):
-            forward(*pieces[p + lag])
+        fac_all(f, c).wait_recv()
+        if p + ahead < len(pieces):
+            fac_start(*pieces[p + ahead])
         if c == 0:
             for i in range(1, nsub):
                 tok_copy(f, i).wait()
                 split(f, lax.rem(half + nsub - i, nsub) * rows_dev)
-        fac_all(f, c).wait_recv()
-        if p + ahead < len(pieces):
-            fac_start(*pieces[p + ahead])
+        if lean:
+            arrive(f, c)
         multiply(f, c)
         if c == chunks - 1:
             for i in range(1, nquad):
@@ -459,7 +487,7 @@
     lanes = -(-ntok * local_q // 128) * 128
     lines = -(-2 * topc // 8) * 8
     ngroup = lax.axis_size("groups")
-    chunks = 4
+    chunks = CHUNKS
     dma = pltpu.SemaphoreType.DMA
     vmem = pl.BlockSpec(memory_space=pltpu.VMEM)
     smem = pl.BlockSpec(memory_space=pltpu.SMEM)

time: 179 us -> 53.3 us (0.30)
  Pallas kernels: 178 us -> 51.9 us
    pallas_call x1, Pallas kernels: 168 us -> 41.9 us  [call(): pl.pallas_call(functools.partial(kernel, ntok, nwide, nsub, chunks, lean)...]
where the time goes in v4:
time: 53.3 us; the launch traced here: 53.1 us
  Pallas kernels  51.9 us (97%)
  between operations  0.63 us (1%)
  local copies, waits for them, and re-layouts  0.6 us (1%)
    pallas_call x1, Pallas kernels, call(): pl.pallas_call(functools.partial(kernel, ntok, nwide, nsub, chunks, lean)...  41.9 us
    pallas_call x1, Pallas kernels, on_device(): pl.pallas_call(functools.partial(meta_kernel, ngroup, ntok), out_shape=(j...  9.99 us

profile of v4, /device:TPU:0, one launch (start us, length us, event | category | flops | bytes accessed | tf_op | source)
XLA Modules:
  0.0 53.1 jit_solution(6215009972686910535)
XLA Ops:
  0.0 10.0 %shard_map.82 = (s32[8,128]{1,0:T(8,128)S(1)}, s32[1]{0:T(128)}) custom-call(s32[1,4]{1,0:T(1,128)} %bitcast.5, s32[1,4]{1,0:T(1,128)} %bitcast.8), custom_call_target="tpu_custom_call" | custom-call | tf_op jit(solution)/shard_map/pallas_call | solution.py:496
  10.6 41.9 %conditional.1 = (f32[16,96]{1,0:T(8,128)S(1)}) conditional(s32[]{:T(128)} %bitcast.2, (f32[192,4096]{1,0:T(8,128)}, f32[192,4096]{1,0:T(8,128)}, bf16[4,16,4096]{2,1,0:T(8,128)(2,1)}, bf16[4,16,4096]{2,1,0:T(8,128)(2,1)}, s32[1,4]{1,0:T(1,128)}, /*index=5*/s32[8,128]{1,0:T(8,128)S(1)}, s32[384]{0:T(512)}, s32[8]{0:T(128)}) %tuple.14, ...), branch_computations={%region_0.0_spmd, %region_1.0_spmd} | conditional | bytes 8 | solution.py:548
  10.6 41.9 %branch_1_fun.1 = f32[16,96]{1,0:T(8,128)S(1)} custom-call(f32[192,4096]{1,0:T(8,128)} %get-tuple-element.48.act_hbm, f32[192,4096]{1,0:T(8,128)} %get-tuple-element.49.cot_hbm, bf16[4,16,4096]{2,1,0:T(8,128)(2,1)} %get-tuple-element.50.u_ref, bf16[4,16,4096]{2,1,0:T(8,128)(2,1)} %get-tuple-element.51.v_ref, s32[1,4]{1,0:T(1,128)} %get-tuple-element.52.dest_ref, ...), custom_call_target="tpu_custom_call" | custom-call | tf_op jit(solution)/shard_map/cond/branch_1_fun/pallas_call | solution.py:517
  52.5 0.6 %copy.12 = f32[96,16]{0,1:T(8,128)} copy(f32[96,16]{0,1:T(8,128)S(1)} %bitcast.4) | data formatting | bytes 12288
